TPU v7x, 1024 devices: a whole 8x8x8 slice. The times are simulated.
1024 devices in a mesh: lat: 64 (over z, y), lon: 16 (over x, core).
Axes of the slice: x: 8, y: 8, z: 8, core: 2. Of those that a mesh axis runs over, the one named last changes fastest.
Arguments:
- saved_input: bfloat16 [640, 384, 2048], P('lat', None, 'lon'), may hold values from -0.1875 to 0.1875
- saved_spectra: bfloat16 [384, 384, 2048], P('lat', None, 'lon'), may hold values from -6 to 6
- out_grad: bfloat16 [384, 384, 2048], P('lat', None, 'lon'), may hold values from -0.1875 to 0.1875
- legendre: bfloat16 [384, 384, 640], P('lat'), may hold values from -0.3125 to 0.3125
- spectral_gain: float32 [384, 256], P(None, 'lon'), may hold values from 0.25 to 4
- band_filter: bfloat16 [640, 13], replicated, may hold values from -24 to 24
- band_start: int32 [640], replicated, may hold values from 0 to 638, as said below
- band_width: int32 [640], replicated, may hold values from 2 to 13, as said below
- slot_order: int32 [384], replicated, may hold values from 0 to 383, each once
Outputs:
- input_grad: bfloat16 [640, 384, 2048], P('lat', None, 'lon')
- gain_grad: float32 [384, 256], P(None, 'lon')
- filter_grad: float32 [640, 13], P('lat')
Inputs may be any that keep to these rules, and one draw needn't show every extreme that they name: Row i's support, rows band_start[i] to band_start[i] + band_width[i] - 1, contains i and lies in the grid and within 6 rows of i; every row but the first reaches at least one row below itself. `band_width`: some row's support has exactly 13 rows. `slot_order`: each order stands in exactly one slot.
All inputs are finite; a program needn't handle non-finite values.
Results may differ from a plain program's by a relative error of at most 0.0057.
Values may be sent and summed in bfloat16 or wider, within the bound.
A program may use at most 64 MiB of HBM per device.

v0:
```python
import jax
import jax.numpy as jnp
from jax import lax
from jax.sharding import PartitionSpec as P


def padded(cells, sides, width):
    for axis, dim in sides:
        count = lax.axis_size(axis)
        ends = count - 1
        head = lax.slice_in_dim(cells, 0, width, axis=dim)
        tail = lax.slice_in_dim(cells, cells.shape[dim] - width, cells.shape[dim], axis=dim)
        cells = jnp.concatenate(
            [
                lax.ppermute(tail, axis, [(i, (i + 1) % count) for i in range(ends)]),
                cells,
                lax.ppermute(head, axis, [((i + 1) % count, i) for i in range(ends)]),
            ],
            axis=dim,
        )
    return cells


def band_matrix(
    band_filter, band_start, band_width, target_first, target_count, source_first, source_count
):
    row_total = band_start.shape[0]
    tap_count = band_filter.shape[1]
    tap_reach = (tap_count - 1) // 2
    source_rows = source_first + jnp.arange(source_count, dtype=jnp.int32)
    inside = (source_rows >= 0) & (source_rows < row_total)
    clipped = jnp.clip(source_rows, 0, row_total - 1)
    starts = jnp.take(band_start, clipped)
    widths = jnp.take(band_width, clipped)
    rows_filter = jnp.take(band_filter, clipped, axis=0)
    target_rows = target_first + jnp.arange(target_count, dtype=jnp.int32)
    row_gap = target_rows[:, None] - source_rows[None, :]
    matrix = jnp.zeros((target_count, source_count), jnp.bfloat16)
    for offset in range(tap_count):
        tap_index = source_rows + offset - tap_reach - starts
        is_valid = inside & (tap_index >= 0) & (tap_index < widths)
        tap_value = jnp.take_along_axis(
            rows_filter, jnp.clip(tap_index, 0, tap_count - 1)[:, None], axis=1
        )[:, 0]
        tap_value = jnp.where(is_valid, tap_value, jnp.zeros_like(tap_value))
        matrix = jnp.where(row_gap == offset - tap_reach, tap_value[None, :], matrix)
    return matrix


def band_pick(gram_block, starts, widths, column_first, tap_count):
    tap_range = jnp.arange(tap_count, dtype=jnp.int32)
    column_index = starts[:, None] + tap_range[None, :] - column_first
    column_index = jnp.clip(column_index, 0, gram_block.shape[1] - 1)
    picked = jnp.take_along_axis(gram_block, column_index, axis=1)
    return jnp.where(tap_range[None, :] < widths[:, None], picked, 0.0)


def per_device(
    saved_input,
    saved_spectra,
    out_grad,
    legendre,
    spectral_gain,
    band_filter,
    band_start,
    band_width,
    slot_order,
):
    rows_local = saved_input.shape[0]
    order_total = saved_input.shape[1]
    slots_local = out_grad.shape[0]
    degree_total = out_grad.shape[1]
    lane_count = out_grad.shape[2]
    tap_count = band_filter.shape[1]
    reach_rows = (tap_count - 1) // 2
    per_channel = lane_count // spectral_gain.shape[1]
    lat_place = lax.axis_index("lat")
    own_orders = lax.dynamic_slice_in_dim(slot_order, lat_place * slots_local, slots_local)
    degrees = jnp.arange(degree_total, dtype=jnp.int32)
    keep_mask = (degrees[None, :] >= own_orders[:, None]).astype(jnp.float32)
    masked = out_grad.astype(jnp.float32) * keep_mask[:, :, None]
    gain_terms = jnp.sum(
        (masked * saved_spectra.astype(jnp.float32)).reshape(
            slots_local, degree_total, -1, per_channel
        ),
        axis=(0, 3),
    )
    gain_grad = lax.psum(gain_terms, "lat")
    lane_gain = jnp.repeat(spectral_gain, per_channel, axis=1)
    spec_grad = (masked * lane_gain[None]).astype(jnp.bfloat16)
    slot_grad = jnp.einsum(
        "kli,kln->ikn", legendre, spec_grad, preferred_element_type=jnp.float32
    ).astype(jnp.bfloat16)
    slot_of = (
        jnp.zeros((order_total,), jnp.int32)
        .at[slot_order]
        .set(jnp.arange(order_total, dtype=jnp.int32))
    )
    wide_input = padded(saved_input, (("lat", 0),), reach_rows)
    received = lax.all_to_all(slot_grad, "lat", split_axis=0, concat_axis=1, tiled=True)
    lat_grad = jnp.take(received, slot_of, axis=1)
    wide_grad = padded(lat_grad, (("lat", 0),), reach_rows)
    first_row = lat_place * rows_local
    band_block = band_matrix(
        band_filter,
        band_start,
        band_width,
        first_row,
        rows_local,
        first_row - reach_rows,
        rows_local + 2 * reach_rows,
    )
    input_grad = jnp.einsum(
        "je,emn->jmn", band_block, wide_grad, preferred_element_type=jnp.float32
    ).astype(jnp.bfloat16)
    gram_block = jnp.einsum("imn,emn->ie", lat_grad, wide_input, preferred_element_type=jnp.float32)
    local_starts = lax.dynamic_slice_in_dim(band_start, first_row, rows_local)
    local_widths = lax.dynamic_slice_in_dim(band_width, first_row, rows_local)
    filter_part = band_pick(
        gram_block, local_starts, local_widths, first_row - reach_rows, tap_count
    )
    filter_grad = lax.psum(filter_part, "lon")
    return (input_grad, gain_grad, filter_grad)


def solution(mesh):
    return jax.shard_map(
        per_device,
        mesh=mesh,
        in_specs=(
            P("lat", None, "lon"),
            P("lat", None, "lon"),
            P("lat", None, "lon"),
            P("lat", None, None),
            P(None, "lon"),
            P(),
            P(),
            P(),
            P(),
        ),
        out_specs=(P("lat", None, "lon"), P(None, "lon"), P("lat", None)),
        check_vma=False,
    )
```

profile of v0, /device:TPU:1, one launch (start us, length us, event | category | flops | bytes accessed | tf_op | source)
XLA Modules:
  0.0 419.5 jit_solution(13356119793456495606)
XLA Ops:
  2.5 3.2 fusion.15
  5.8 2.8 copy.32
  8.5 24.2 %all-to-all-start = ((bf16[640,6,128]{2,1,0:T(8,128)(2,1)}), bf16[640,6,128]{2,1,0:T(8,128)(2,1)}, u32[]{:S(2)}, u32[]{:S(2)}) async-start(bf16[640,6,128]{2,1,0:T(8,128)(2,1)} %copy.32), calls=%async_computation | async-start | bytes 2621440 | tf_op jit(solution)/shard_map/all_to_all | solution.py:100
  32.8 2.4 fusion.118
  35.1 3.7 collective-permute-start.2
  56.9 1.6 gather_fusion.10
  59.9 1.5 gather_fusion.8
  61.4 1.5 gather_fusion.7
  66.5 2.1 multiply_reduce_fusion
  70.4 2.9 scatter_custom_fusion
  76.6 2.8 copy.45
  79.4 3.5 gather_fusion.1
  82.9 2.4 select_bitcast_fusion
  88.7 5.5 %collective-permute-start = (bf16[6,384,128]{2,1,0:T(8,128)(2,1)S(1)}, bf16[6,384,128]{2,1,0:T(8,128)(2,1)}, u32[]{:S(2)}, u32[]{:S(2)}) collective-permute-start(bf16[6,384,128]{2,1,0:T(8,128)(2,1)S(1)} %copy.35), channel_id=1, source_target_pairs={{0,16},{16,32},{32,48},{48,64},{64,80},{80,96},{96,112},{112,128},... | collective-permute-start | bytes 1769480 | tf_op jit(solution)/shard_map/ppermute | solution.py:15
  95.4 1.9 copy.41
  97.3 225.9 %psum.14 = f32[384,16]{0,1:T(8,128)} all-reduce(f32[384,16]{0,1:T(8,128)} %bitcast_reduce_fusion), channel_id=1, replica_groups=mesh['lat'=64,'lon'=16] {'lat'}, use_global_device_ids=true, to_apply=%region_3.6 | all-reduce | flops 6144 | bytes 49152 | tf_op jit(solution)/shard_map/psum | solution.py:88
  323.2 1.6 copy.40
  324.8 1.5 copy.42
  326.3 2.4 fusion.16
  328.6 2.2 gather_fusion.2
  332.3 80.8 %psum.15 = f32[10,13]{1,0:T(8,128)} all-reduce(f32[10,13]{1,0:T(8,128)} %select_select_fusion), channel_id=1, replica_groups=mesh['lat'=64,'lon'=16] {'lon'}, use_global_device_ids=true, to_apply=%region_4.7 | all-reduce | flops 130 | bytes 1040 | tf_op jit(solution)/shard_map/psum | solution.py:122
  413.1 1.6 copy.38
  414.7 1.5 copy.37
  416.2 2.1 fusion.12
  (96 shorter events, 37.2 us)
Async XLA Ops:
  0.6 1.9 copy-start
  1.6 4.1 copy-start.9
  8.5 68.1 %all-to-all-start = ((bf16[640,6,128]{2,1,0:T(8,128)(2,1)}), bf16[640,6,128]{2,1,0:T(8,128)(2,1)}, u32[]{:S(2)}, u32[]{:S(2)}) async-start(bf16[640,6,128]{2,1,0:T(8,128)(2,1)} %copy.32), calls=%async_computation | async-start | bytes 2621440 | tf_op jit(solution)/shard_map/all_to_all | solution.py:100
  32.7 7.4 %copy-start.1 = (s32[640]{0:T(1024)S(1)}, s32[640]{0:T(1024)}, u32[]{:S(2)}) copy-start(s32[640]{0:T(1024)} %param.19) | copy-start | bytes 7684
  32.8 11.6 %copy-start.10 = (bf16[640,13]{0,1:T(8,128)(2,1)S(1)}, bf16[640,13]{0,1:T(8,128)(2,1)}, u32[]{:S(2)}) copy-start(bf16[640,13]{0,1:T(8,128)(2,1)} %param.18) | copy-start | bytes 49924
  32.8 13.1 %copy-start.2 = (s32[640]{0:T(1024)S(1)}, s32[640]{0:T(1024)}, u32[]{:S(2)}) copy-start(s32[640]{0:T(1024)} %param.20) | copy-start | bytes 7684
  35.1 288.1 %collective-permute-start.2 = (bf16[6,384,128]{2,1,0:T(8,128)(2,1)}, bf16[6,384,128]{2,1,0:T(8,128)(2,1)}, u32[]{:S(2)}, u32[]{:S(2)}) collective-permute-start(bf16[6,384,128]{2,1,0:T(8,128)(2,1)} %get-tuple-element.18), channel_id=1, source_target_pairs={{0,16},{16,32},{32,48},{48,64},{64,80},{80,96},{96,112},{112,128},... | collective-permute-start | bytes 1769480 | tf_op jit(solution)/shard_map/ppermute | solution.py:15
  38.8 286.0 %collective-permute-start.3 = (bf16[6,384,128]{2,1,0:T(8,128)(2,1)}, bf16[6,384,128]{2,1,0:T(8,128)(2,1)}, u32[]{:S(2)}, u32[]{:S(2)}) collective-permute-start(bf16[6,384,128]{2,1,0:T(8,128)(2,1)} %get-tuple-element.19), channel_id=1, source_target_pairs={{16,0},{32,16},{48,32},{64,48},{80,64},{96,80},{112,96},{128,112},... | collective-permute-start | bytes 1769480 | tf_op jit(solution)/shard_map/ppermute | solution.py:17
  40.9 3.7 copy-start.11
  54.1 8.9 %copy-start.8 = (s32[22]{0:T(128)S(1)}, s32[22]{0:T(128)}, u32[]{:S(2)}) copy-start(s32[22]{0:T(128)} %or_bitcast_fusion.11) | copy-start | bytes 268
  56.9 9.6 %copy-start.7 = (bf16[6,384,128]{2,1,0:T(8,128)(2,1)S(1)}, bf16[6,384,128]{2,1,0:T(8,128)(2,1)}, u32[]{:S(2)}) copy-start(bf16[6,384,128]{2,1,0:T(8,128)(2,1)} %param.15) | copy-start | bytes 1769476
  85.3 1.2 copy-start.3
  86.5 8.9 %copy-start.6 = (bf16[10,384,128]{2,1,0:T(8,128)(2,1)S(1)}, bf16[10,384,128]{2,1,0:T(8,128)(2,1)}, u32[]{:S(2)}) copy-start(bf16[10,384,128]{2,1,0:T(8,128)(2,1)} %param.13) | copy-start | bytes 2949124
  87.4 325.6 %collective-permute-start.1 = (bf16[6,384,128]{2,1,0:T(8,128)(2,1)}, bf16[6,384,128]{2,1,0:T(8,128)(2,1)}, u32[]{:S(2)}, u32[]{:S(2)}) collective-permute-start(bf16[6,384,128]{2,1,0:T(8,128)(2,1)} %copy.36), channel_id=1, source_target_pairs={{16,0},{32,16},{48,32},{64,48},{80,64},{96,80},{112,96},{128,112},... | collective-permute-start | bytes 1769480 | tf_op jit(solution)/shard_map/ppermute | solution.py:17
  88.7 326.0 %collective-permute-start = (bf16[6,384,128]{2,1,0:T(8,128)(2,1)S(1)}, bf16[6,384,128]{2,1,0:T(8,128)(2,1)}, u32[]{:S(2)}, u32[]{:S(2)}) collective-permute-start(bf16[6,384,128]{2,1,0:T(8,128)(2,1)S(1)} %copy.35), channel_id=1, source_target_pairs={{0,16},{16,32},{32,48},{48,64},{64,80},{80,96},{96,112},{112,128},... | collective-permute-start | bytes 1769480 | tf_op jit(solution)/shard_map/ppermute | solution.py:15
  323.2 3.1 copy-start.4
  330.9 85.3 %copy-start.12 = (bf16[22]{0:T(256)(128)(2,1)S(1)}, bf16[22]{0:T(256)(128)(2,1)}, u32[]{:S(2)}) copy-start(bf16[22]{0:T(256)(128)(2,1)} %get-tuple-element.20) | copy-start | bytes 136
  331.0 85.2 %copy-start.13 = (bf16[22]{0:T(256)(128)(2,1)S(1)}, bf16[22]{0:T(256)(128)(2,1)}, u32[]{:S(2)}) copy-start(bf16[22]{0:T(256)(128)(2,1)} %get-tuple-element.21) | copy-start | bytes 136
  413.1 3.1 copy-start.5
where the time goes:
time: 420 us; the launch traced here: 419 us
  blocking collectives  307 us (73%)
  local copies, waits for them, and re-layouts  53.4 us (13%)
  starting transfers between devices  35.9 us (9%)
  other arithmetic  14.9 us (4%)
  matrix products  7.69 us (2%)
    psum x1, blocking collectives, per_device(): gain_grad = lax.psum(gain_terms, 'lat')  226 us
    psum x1, blocking collectives, per_device(): filter_grad = lax.psum(filter_part, 'lon')  80.8 us
    all_to_all x1, starting transfers between devices, per_device(): lax.all_to_all(slot_grad, 'lat', split_axis=0, concat_axis=1, tiled=True)  24.2 us
    gather x13, local copies, waits for them, and re-layouts, band_matrix(): jnp.take_along_axis(rows_filter, jnp.clip(tap_index, 0, tap_count - 1)[:,...  18.7 us
    ppermute x2, starting transfers between devices, padded(): lax.ppermute(tail, axis, [(i, (i + 1) % count) for i in range(ends)])  9.12 us
  transfers between devices with their start and end apart: 5, of which 0 were waited for; matrix products, arithmetic and copies ran while one was open for 15% of the time, Pallas kernels for 0%

commit v1 on v0

v1 whole, which is shorter than its diff:
```python
import functools
import jax
import jax.numpy as jnp
from jax import lax
from jax.sharding import PartitionSpec as P
from jax.experimental import pallas as pl
from jax.experimental.pallas import tpu as pltpu

MESH = pl.DeviceIdType.MESH
HIGHEST = lax.Precision.HIGHEST
F32 = jnp.float32
BF16 = jnp.bfloat16
I32 = jnp.int32

RING = 8
SLOTS = 2
CHUNKS = 3
ORIENT = ("y", "z", "z")
TILE = RING * SLOTS
REACH = 6
ROWS = 10
PLANE = RING * ROWS
WINDOW = 24
FAR_FIRST = (4, 3, 5, 2, 6, 1, 7)


def iota(shape, dim):
    return lax.broadcasted_iota(I32, shape, dim)


def dot(a, b, contract=((1,), (0,)), precision=None):
    return lax.dot_general(
        a, b, (contract, ((), ())), preferred_element_type=F32, precision=precision
    )


def kernel(
    lon_count,
    sv_hbm,
    sp_hbm,
    og_hbm,
    leg_hbm,
    gain_ref,
    filt_ref,
    start_ref,
    width_ref,
    order_ref,
    order_row_ref,
    ig_hbm,
    gg_ref,
    fg_ref,
    sv,
    sp,
    og,
    leg,
    sent,
    got,
    turned,
    window,
    sv_slots,
    ig_slots,
    pick,
    out_rows,
    gain_mine,
    gain_got,
    gain_part,
    gain_got2,
    gain_all,
    filt_mine,
    filt_got,
    filt_sum,
    filt_all,
    load_sems,
    own_sems,
    out_sems,
    p1_send,
    p1_recv,
    p2_send,
    p2_recv,
    halo_send,
    halo_recv,
    g1_send,
    g1_recv,
    g2_send,
    g2_recv,
    g3_send,
    g3_recv,
    f1_send,
    f1_recv,
    f2_send,
    f2_recv,
):
    p = lax.axis_index("lat")
    q = lax.axis_index("lon")
    z, y = p // RING, lax.rem(p, RING)
    lat_count = RING * RING

    def z_peer(d):
        return lax.rem(z + d, RING) * RING + y

    def y_peer(d):
        return z * RING + lax.rem(y + d, RING)

    peer_of = {"z": z_peer, "y": y_peer}
    place_of = {"z": z, "y": y}
    other = {"z": "y", "y": "z"}
    up = lax.rem(p + 1, lat_count)
    down = lax.rem(p + lat_count - 1, lat_count)

    def remote(src, dst, s, r, lat):
        return pltpu.make_async_remote_copy(
            src_ref=src,
            dst_ref=dst,
            send_sem=s,
            recv_sem=r,
            device_id={"lat": lat},
            device_id_type=MESH,
        )

    loads = {}

    def load(name, index, src, dst):
        cp = pltpu.make_async_copy(src, dst, load_sems.at[index])
        cp.start()
        loads[name] = cp

    for c in range(CHUNKS):
        part = pl.ds(SLOTS * c, SLOTS)
        load(("og", c), 2 * c, og_hbm.at[part], og.at[part])
        load(("leg", c), 2 * c + 1, leg_hbm.at[part], leg.at[part])
    load("sp", 6, sp_hbm, sp)
    load("sv", 7, sv_hbm, sv)

    barrier = pltpu.get_barrier_semaphore()
    for d in range(1, RING):
        for axis in ("z", "y"):
            pl.semaphore_signal(
                barrier, inc=1, device_id={"lat": peer_of[axis](d)}, device_id_type=MESH
            )
    for lat in (up, down):
        pl.semaphore_signal(barrier, inc=1, device_id={"lat": lat}, device_id_type=MESH)
    for d in range(1, lon_count):
        pl.semaphore_signal(
            barrier,
            inc=1,
            device_id={"lon": lax.rem(q + d, lon_count)},
            device_id_type=MESH,
        )

    degrees = sp.shape[1]
    lanes = sp.shape[2]
    channels = gain_ref.shape[1]
    per_channel = lanes // channels
    lat_rows = lat_count * ROWS

    spread = (iota((channels, lanes), 1) // per_channel == iota((channels, lanes), 0)).astype(F32)
    lane_gain = dot(gain_ref[...], spread, precision=HIGHEST)

    degree = iota((degrees, lanes), 0)

    def turn_rows():
        row = iota((lat_rows, 128), 0)
        tens = lax.shift_right_logical(row * 6554, 16)
        rest = row - tens * ROWS
        major = lax.shift_right_logical(tens, 3)
        minor = tens & 7
        target = minor * PLANE + major * ROWS + rest
        lane = iota((lat_rows, 128), 1)
        return jnp.concatenate(
            [(target == lane + 128 * b).astype(BF16) for b in range(lat_rows // 128)], axis=1
        )

    rows_turned = turn_rows() if "y" in ORIENT else None

    def make_chunk(c):
        loads["og", c].wait()
        loads["leg", c].wait()
        for s in range(SLOTS):
            k = SLOTS * c + s
            keep = degree >= order_ref[p * (SLOTS * CHUNKS) + k]
            masked = jnp.where(keep, og[k].astype(F32), 0.0)
            spec = (masked * lane_gain).astype(BF16)
            grad = dot(leg[k], spec, ((0,), (0,))).astype(BF16)
            if ORIENT[c] == "y":
                grad = dot(rows_turned, grad).astype(BF16)
            for t in range(RING):
                sent[c, t, s] = grad[t * PLANE : (t + 1) * PLANE]

    phase1 = {}
    phase2 = {}
    halo = {}

    def send_phase1(c):
        axis = ORIENT[c]
        me = place_of[axis]
        cps = []
        for n, d in enumerate(FAR_FIRST):
            target = lax.rem(me + d, RING)
            cp = remote(
                sent.at[c, target], got.at[c, me], p1_send.at[c, n], p1_recv.at[c, n], peer_of[axis](d)
            )
            cp.start()
            cps.append(cp)
        got[c, me] = sent[c, me]
        phase1[c] = cps

    a, b = iota((256, 256), 0), iota((256, 256), 1)
    swap = ((a & 15) * 16 + lax.shift_right_logical(a, 4) == b).astype(BF16)

    def turn(c):
        for cp in phase1[c]:
            cp.wait_recv()
        for blk in range(PLANE // 16):
            x = got[c, :, :, blk * 16 : (blk + 1) * 16, :].reshape(256, lanes)
            turned[c, blk * 16 : (blk + 1) * 16] = dot(swap, x).astype(BF16).reshape(16, TILE, lanes)

    def send_phase2(c):
        axis = other[ORIENT[c]]
        me = place_of[axis]
        cps = []
        for n, d in enumerate(FAR_FIRST):
            target = lax.rem(me + d, RING)
            cp = remote(
                turned.at[c, pl.ds(target * ROWS, ROWS)],
                window.at[c, me, pl.ds(REACH, ROWS)],
                p2_send.at[c, n],
                p2_recv.at[c, n],
                peer_of[axis](d),
            )
            cp.start()
            cps.append(cp)
        window[c, me, REACH : REACH + ROWS] = turned[c, pl.ds(me * ROWS, ROWS)]
        phase2[c] = cps

    def send_halo(c):
        for cp in phase2[c]:
            cp.wait_recv()
        cps = [
            remote(
                window.at[c, :, pl.ds(ROWS, REACH)],
                window.at[c, :, pl.ds(0, REACH)],
                halo_send.at[c, 0],
                halo_recv.at[c, 0],
                up,
            ),
            remote(
                window.at[c, :, pl.ds(REACH, REACH)],
                window.at[c, :, pl.ds(REACH + ROWS, REACH)],
                halo_send.at[c, 1],
                halo_recv.at[c, 1],
                down,
            ),
        ]
        for cp in cps:
            cp.start()
        halo[c] = cps

    make_chunk(0)
    pl.semaphore_wait(barrier, 2 * (RING - 1) + 2 + lon_count - 1)
    send_phase1(0)
    make_chunk(1)
    send_phase1(1)
    make_chunk(2)

    loads["sp"].wait()
    total = jnp.zeros((degrees, lanes), F32)
    for k in range(SLOTS * CHUNKS):
        keep = degree >= order_ref[p * (SLOTS * CHUNKS) + k]
        masked = jnp.where(keep, og[k].astype(F32), 0.0)
        total = total + masked * sp[k].astype(F32)
    groups = degrees // 64
    packed = jnp.zeros((64, 128), F32)
    lane_from, lane_to = iota((lanes, 128), 0), iota((lanes, 128), 1)
    for g in range(groups):
        fold = (lane_from // per_channel + channels * g == lane_to).astype(F32)
        packed = packed + dot(total[64 * g : 64 * (g + 1)], fold, precision=HIGHEST)
    gain_mine[...] = packed.reshape(RING, 8, 128)
    gain1 = []
    for n, d in enumerate(FAR_FIRST):
        cp = remote(
            gain_mine.at[lax.rem(z + d, RING)], gain_got.at[z], g1_send.at[n], g1_recv.at[n], z_peer(d)
        )
        cp.start()
        gain1.append(cp)
    gain_got[z] = gain_mine[z]

    k = iota((degrees, degrees), 0)
    lat_of = lax.shift_right_logical(k * 10923, 16)
    rest = k - lat_of * (SLOTS * CHUNKS)
    chunk_of, s_of = lax.shift_right_logical(rest, 1), rest & 1
    z_of, y_of = lax.shift_right_logical(lat_of, 3), lat_of & 7
    z_first = y_of * TILE + z_of * SLOTS + s_of
    y_first = z_of * TILE + y_of * SLOTS + s_of
    column = z_first
    for c in range(CHUNKS):
        if ORIENT[c] == "y":
            column = jnp.where(chunk_of == c, y_first, column)
    column = column + chunk_of * 128
    arrive = (column == iota((degrees, degrees), 1)).astype(F32)
    order_row = jnp.broadcast_to(order_row_ref[...].astype(F32), (8, degrees))
    order_arrive = dot(order_row, arrive, precision=HIGHEST)[0:1]
    pick_f32 = (
        iota((degrees, degrees), 0).astype(F32) == jnp.broadcast_to(order_arrive, (degrees, degrees))
    ).astype(F32)
    pick[...] = pick_f32.astype(BF16)
    pick_t = pick_f32.T.astype(BF16)

    turn(1)
    send_phase2(1)
    send_phase1(2)

    loads["sv"].wait()
    for j in range(0, ROWS, 2):
        pair = jnp.concatenate([sv[j], sv[j + 1]], axis=1)
        moved = dot(pick_t, pair).astype(BF16)
        sv_slots[j] = moved[:, :lanes]
        sv_slots[j + 1] = moved[:, lanes:]

    turn(0)

    first = p * ROWS
    e_row = iota((WINDOW, 128), 0)
    lane = iota((WINDOW, 128), 1)
    starts = jnp.zeros((WINDOW, 128), I32)
    widths = jnp.zeros((WINDOW, 128), I32)
    for e in range(ROWS + 2 * REACH):
        row = jnp.clip(first - REACH + e, 0, lat_rows - 1)
        starts = jnp.where(e_row == e, start_ref[row], starts)
        widths = jnp.where(e_row == e, width_ref[row], widths)
    row_e = e_row + (first - REACH)
    inside = (row_e >= 0) & (row_e < lat_rows) & (e_row < ROWS + 2 * REACH)
    widths = jnp.where(inside, widths, 0)
    row_pick = (iota((WINDOW, lat_rows), 1) == iota((WINDOW, lat_rows), 0) + (first - REACH)).astype(BF16)
    taps = dot(row_pick, filt_ref[...])
    tap_count = taps.shape[1]
    tap = lane + first - starts
    band = jnp.zeros((WINDOW, 128), F32)
    for t in range(tap_count):
        hit = (tap == t) & (t < widths)
        band = jnp.where(hit, jnp.broadcast_to(taps[:, t : t + 1], (WINDOW, 128)), band)
    pick_j = (lax.shift_right_logical(iota((ROWS * TILE, 128), 0), 4) == iota((ROWS * TILE, 128), 1)).astype(BF16)
    pick_e = (lax.shift_right_logical(iota((WINDOW, WINDOW * TILE), 1), 4) == iota((WINDOW, WINDOW * TILE), 0)).astype(BF16)
    wide = dot(pick_j, band.astype(BF16), ((1,), (1,))).astype(BF16)
    wide = dot(wide, pick_e)
    same_slot = (iota((ROWS * TILE, WINDOW * TILE), 0) & 15) == (iota((ROWS * TILE, WINDOW * TILE), 1) & 15)
    band_wide = jnp.where(same_slot, wide, 0.0).astype(BF16)

    for c in range(CHUNKS):
        window[c, :, ROWS + 2 * REACH : WINDOW] = jnp.zeros(
            (RING, WINDOW - ROWS - 2 * REACH, TILE, lanes), BF16
        )

    turn(2)
    send_phase2(2)
    send_phase2(0)

    for cp in gain1:
        cp.wait_recv()
    gain_part[...] = jnp.sum(gain_got[...], axis=0)
    gain2 = []
    for n, d in enumerate(FAR_FIRST):
        cp = remote(gain_part, gain_got2.at[y], g2_send.at[n], g2_recv.at[n], y_peer(d))
        cp.start()
        gain2.append(cp)
    gain_got2[y] = gain_part[...]

    gram = jnp.zeros((WINDOW * TILE, ROWS * TILE), F32)

    def finish_chunk(c, gram):
        for cp in halo[c]:
            cp.wait_recv()
        tiles, sides = [], []
        for t in range(RING):
            x = window[c, t].reshape(WINDOW * TILE, lanes)
            lo = c * 128 + t * TILE
            ig_slots[:, lo : lo + TILE, :] = dot(band_wide, x).astype(BF16).reshape(ROWS, TILE, lanes)
            tiles.append(x)
            sides.append(sv_slots[:, lo : lo + TILE, :].reshape(ROWS * TILE, lanes))
        return gram + dot(jnp.concatenate(tiles, axis=1), jnp.concatenate(sides, axis=1), ((1,), (1,)))

    send_halo(1)
    gram = finish_chunk(1, gram)
    send_halo(0)
    for cp in gain2:
        cp.wait_recv()
    gain_mine_sum = jnp.sum(gain_got2[...], axis=0)
    gain_all[z] = gain_mine_sum
    gain3 = []
    for n, d in enumerate(FAR_FIRST):
        cp = remote(gain_all.at[z], gain_all.at[z], g3_send.at[n], g3_recv.at[n], z_peer(d))
        cp.start()
        gain3.append(cp)
    send_halo(2)
    gram = finish_chunk(0, gram)
    for cp in gain3:
        cp.wait_recv()
    summed = gain_all[...].reshape(64, 128)
    for g in range(groups):
        gg_ref[64 * g : 64 * (g + 1), :] = summed[:, channels * g : channels * (g + 1)]
    gram = finish_chunk(2, gram)

    diagonal = (iota(gram.shape, 0) & 15) == (iota(gram.shape, 1) & 15)
    gram = jnp.where(diagonal, gram, 0.0)
    by_j = (lax.shift_right_logical(iota((ROWS * TILE, 128), 0), 4) == iota((ROWS * TILE, 128), 1)).astype(F32)
    by_e = (lax.shift_right_logical(iota((WINDOW, WINDOW * TILE), 1), 4) == iota((WINDOW, WINDOW * TILE), 0)).astype(F32)
    small = dot(dot(by_e, gram, precision=HIGHEST), by_j, precision=HIGHEST)
    part = jnp.zeros((WINDOW, 128), F32)
    for j in range(ROWS):
        hit = (lane + starts == first + j) & (lane < widths)
        part = part + jnp.where(hit, jnp.broadcast_to(small[:, j : j + 1], (WINDOW, 128)), 0.0)
    filt_mine[...] = part
    filt1 = [
        remote(filt_mine, filt_got.at[0], f1_send.at[0], f1_recv.at[0], up),
        remote(filt_mine, filt_got.at[1], f1_send.at[1], f1_recv.at[1], down),
    ]
    for cp in filt1:
        cp.start()

    writes = []
    for j in range(0, ROWS, 2):
        if j == 4:
            for cp in filt1:
                cp.wait_recv()
            filt_sum[...] = jnp.zeros(filt_sum.shape, F32)
            filt_sum[0:ROWS] = filt_mine[REACH : REACH + ROWS]
            filt_sum[0:REACH] += filt_got[0, REACH + ROWS : ROWS + 2 * REACH]
            filt_sum[ROWS - REACH : ROWS] += filt_got[1, 0:REACH]
            filt_all[q] = filt_sum[...]
            filt2 = []
            for d in range(1, lon_count):
                cp = pltpu.make_async_remote_copy(
                    src_ref=filt_all.at[q],
                    dst_ref=filt_all.at[q],
                    send_sem=f2_send.at[d - 1],
                    recv_sem=f2_recv.at[d - 1],
                    device_id={"lon": lax.rem(q + d, lon_count)},
                    device_id_type=MESH,
                )
                cp.start()
                filt2.append(cp)
        pair = jnp.concatenate([ig_slots[j], ig_slots[j + 1]], axis=1)
        moved = dot(pick[...], pair).astype(BF16)
        out_rows[j] = moved[:, :lanes]
        out_rows[j + 1] = moved[:, lanes:]
        cp = pltpu.make_async_copy(
            out_rows.at[pl.ds(j, 2)], ig_hbm.at[pl.ds(j, 2)], out_sems.at[j // 2]
        )
        cp.start()
        writes.append(cp)

    for cp in filt2:
        cp.wait_recv()
    fg_ref[...] = jnp.sum(filt_all[...], axis=0)[:ROWS, :tap_count]
    for cps in [*phase1.values(), *phase2.values(), *halo.values(), gain1, gain2, gain3, filt1, filt2]:
        for cp in cps:
            cp.wait_send()
    for cp in writes:
        cp.wait()


def per_device(sv, sp, og, leg, gain, filt, start, width, order):
    lon_count = lax.axis_size("lon")
    slots, degrees, lanes = sp.shape
    rows, orders = sv.shape[0], sv.shape[1]
    lat_rows, tap_count = filt.shape
    any_space = pl.BlockSpec(memory_space=pl.ANY)
    vmem = pl.BlockSpec(memory_space=pltpu.VMEM)
    smem = pl.BlockSpec(memory_space=pltpu.SMEM)
    dma = pltpu.SemaphoreType.DMA
    peers = RING - 1
    return pl.pallas_call(
        functools.partial(kernel, lon_count),
        out_shape=(
            jax.ShapeDtypeStruct(sv.shape, BF16),
            jax.ShapeDtypeStruct(gain.shape, F32),
            jax.ShapeDtypeStruct((rows, tap_count), F32),
        ),
        in_specs=[any_space] * 4 + [vmem] * 2 + [smem] * 3 + [vmem],
        out_specs=(any_space, vmem, vmem),
        scratch_shapes=[
            pltpu.VMEM(sv.shape, BF16),
            pltpu.VMEM(sp.shape, BF16),
            pltpu.VMEM(og.shape, BF16),
            pltpu.VMEM(leg.shape, BF16),
            pltpu.VMEM((CHUNKS, RING, SLOTS, PLANE, lanes), BF16),
            pltpu.VMEM((CHUNKS, RING, SLOTS, PLANE, lanes), BF16),
            pltpu.VMEM((CHUNKS, PLANE, TILE, lanes), BF16),
            pltpu.VMEM((CHUNKS, RING, WINDOW, TILE, lanes), BF16),
            pltpu.VMEM((rows, orders, lanes), BF16),
            pltpu.VMEM((rows, orders, lanes), BF16),
            pltpu.VMEM((orders, orders), BF16),
            pltpu.VMEM((rows, orders, lanes), BF16),
            pltpu.VMEM((RING, 8, 128), F32),
            pltpu.VMEM((RING, 8, 128), F32),
            pltpu.VMEM((8, 128), F32),
            pltpu.VMEM((RING, 8, 128), F32),
            pltpu.VMEM((RING, 8, 128), F32),
            pltpu.VMEM((WINDOW, 128), F32),
            pltpu.VMEM((2, WINDOW, 128), F32),
            pltpu.VMEM((16, 128), F32),
            pltpu.VMEM((lon_count, 16, 128), F32),
            dma((8,)),
            dma((1,)),
            dma((rows // 2,)),
            dma((CHUNKS, peers)),
            dma((CHUNKS, peers)),
            dma((CHUNKS, peers)),
            dma((CHUNKS, peers)),
            dma((CHUNKS, 2)),
            dma((CHUNKS, 2)),
            dma((peers,)),
            dma((peers,)),
            dma((peers,)),
            dma((peers,)),
            dma((peers,)),
            dma((peers,)),
            dma((2,)),
            dma((2,)),
            dma((lon_count - 1,)),
            dma((lon_count - 1,)),
        ],
        compiler_params=pltpu.CompilerParams(
            collective_id=0, has_side_effects=True, vmem_limit_bytes=48 * 2**20
        ),
        name="backward",
    )(sv, sp, og, leg, gain, filt, start, width, order, order.reshape(1, -1))


def solution(mesh):
    return jax.shard_map(
        per_device,
        mesh=mesh,
        in_specs=(
            P("lat", None, "lon"),
            P("lat", None, "lon"),
            P("lat", None, "lon"),
            P("lat", None, None),
            P(None, "lon"),
            P(),
            P(),
            P(),
            P(),
        ),
        out_specs=(P("lat", None, "lon"), P(None, "lon"), P("lat", None)),
        check_vma=False,
    )
```

time: 420 us -> 95.1 us (0.23)
  blocking collectives: 307 us -> 0 us
  Pallas kernels: 0 us -> 83.8 us
  local copies, waits for them, and re-layouts: 53.4 us -> 10.1 us
  starting transfers between devices: 35.9 us -> 0 us
  other arithmetic: 14.9 us -> 0 us
  matrix products: 7.69 us -> 0 us
    psum x2 -> x0, blocking collectives: 307 us -> none  [the longest x1 226 us: per_device(): gain_grad = lax.psum(gain_terms, 'lat')]
    pallas_call x0 -> x1, Pallas kernels: none -> 83.8 us  [per_device(): pl.pallas_call(functools.partial(kernel, lon_count), out_shape=(jax.Shape...]
    gather x20 -> x0, local copies, waits for them, and re-layouts: 26.9 us -> none  [the longest x13 18.7 us: band_matrix(): jnp.take_along_axis(rows_filter, jnp.clip(tap_index, 0, tap_count - 1)[:,...]
    all_to_all x1 -> x0, starting transfers between devices: 24.2 us -> none  [per_device(): lax.all_to_all(slot_grad, 'lat', split_axis=0, concat_axis=1, tiled=True)]
    ppermute x4 -> x0, starting transfers between devices: 11.7 us -> none  [the longest x2 9.12 us: padded(): lax.ppermute(tail, axis, [(i, (i + 1) % count) for i in range(ends)])]
    dot_general x3 -> x0, matrix products: 7.69 us -> none  [the longest x1 3.24 us: per_device(): jnp.einsum('kli,kln->ikn', legendre, spec_grad, preferred_element_type=jn...]
    ppermute x4 -> x0, local copies, waits for them, and re-layouts: 6.13 us -> none  [the longest x2 3.07 us: padded(): lax.ppermute(tail, axis, [(i, (i + 1) % count) for i in range(ends)])]
    select_n x7 -> x0, other arithmetic: 5.93 us -> none  [the longest x2 2.42 us: per_device(): lat_grad = jnp.take(received, slot_of, axis=1)]
  transfers between devices with their start and end apart: 5 -> 0, of which waited for: 0 -> 0; matrix products, arithmetic and copies ran while one was open for 15% -> 0% of each run, Pallas kernels for 0% -> 0%
where the time goes in v1:
time: 95.1 us; the launch traced here: 94.6 us
  Pallas kernels  83.8 us (88%)
  local copies, waits for them, and re-layouts  10.1 us (11%)
    pallas_call x1, Pallas kernels, per_device(): pl.pallas_call(functools.partial(kernel, lon_count), out_shape=(jax.Shape...  83.8 us
    unnamed x16, local copies, waits for them, and re-layouts  8.69 us

profile of v1, /device:TPU:1, one launch (start us, length us, event | category | flops | bytes accessed | tf_op | source)
XLA Modules:
  0.0 94.6 jit_solution(9494041127044879780)
XLA Ops:
  0.6 0.7 reshape.9.order_row_ref
  1.3 0.9 copy.13.filt_ref
  2.2 0.9 copy.12.gain_ref
  3.1 0.0 copy-start
  3.1 1.2 %copy-done = bf16[10,384,128]{2,1,0:T(8,128)(2,1)S(1)} copy-done((bf16[10,384,128]{2,1,0:T(8,128)(2,1)S(1)}, bf16[10,384,128]{2,1,0:T(8,128)(2,1)}, u32[]{:S(2)}) %copy-start) | copy-done | bytes 983064
  4.3 0.0 copy-start.1
  4.3 1.1 %copy-done.1 = bf16[6,384,128]{2,1,0:T(8,128)(2,1)S(1)} copy-done((bf16[6,384,128]{2,1,0:T(8,128)(2,1)S(1)}, bf16[6,384,128]{2,1,0:T(8,128)(2,1)}, u32[]{:S(2)}) %copy-start.1) | copy-done | bytes 589848
  5.4 0.0 copy-start.2
  5.4 1.1 %copy-done.2 = bf16[6,384,128]{2,1,0:T(8,128)(2,1)S(1)} copy-done((bf16[6,384,128]{2,1,0:T(8,128)(2,1)S(1)}, bf16[6,384,128]{2,1,0:T(8,128)(2,1)}, u32[]{:S(2)}) %copy-start.2) | copy-done | bytes 589848
  6.4 0.0 copy-start.3
  6.4 0.7 copy-done.3
  7.1 0.0 copy-start.4
  7.1 0.7 copy-done.4
  7.8 0.0 copy-start.5
  7.8 0.7 copy-done.5
  8.5 83.8 %backward.1 = (bf16[10,384,128]{2,1,0:T(8,128)(2,1)S(1)}, f32[384,16]{1,0:T(8,128)S(1)}, f32[10,13]{1,0:T(8,128)S(1)}) custom-call(bf16[10,384,128]{2,1,0:T(8,128)(2,1)S(1)} %copy-done, bf16[6,384,128]{2,1,0:T(8,128)(2,1)S(1)} %copy-done.1, bf16[6,384,128]{2,1,0:T(8,128)(2,1)S(1)} %copy-done.2, bf16[6,384,640]{2,1,0:T(8,128)(2,1)} %leg_hbm.1, ...), custom_call_target="tpu_custom_call" | custom-call | tf_op jit(solution)/shard_map/backward/pallas_call | solution.py:471
  92.3 0.7 copy.14
  93.0 0.9 copy.17
  94.0 0.6 copy.18
Async XLA Ops:
  3.1 1.2 %copy-start = (bf16[10,384,128]{2,1,0:T(8,128)(2,1)S(1)}, bf16[10,384,128]{2,1,0:T(8,128)(2,1)}, u32[]{:S(2)}) copy-start(bf16[10,384,128]{2,1,0:T(8,128)(2,1)} %sv_hbm.1) | copy-start | bytes 2949124
  4.3 1.1 %copy-start.1 = (bf16[6,384,128]{2,1,0:T(8,128)(2,1)S(1)}, bf16[6,384,128]{2,1,0:T(8,128)(2,1)}, u32[]{:S(2)}) copy-start(bf16[6,384,128]{2,1,0:T(8,128)(2,1)} %sp_hbm.1) | copy-start | bytes 1769476
  5.4 1.1 %copy-start.2 = (bf16[6,384,128]{2,1,0:T(8,128)(2,1)S(1)}, bf16[6,384,128]{2,1,0:T(8,128)(2,1)}, u32[]{:S(2)}) copy-start(bf16[6,384,128]{2,1,0:T(8,128)(2,1)} %og_hbm.1) | copy-start | bytes 1769476
  6.4 0.7 copy-start.3
  7.1 0.7 copy-start.4
  7.8 0.7 copy-start.5

commit v2 on v1

--- a/solution.py
+++ b/solution.py
@@ -15,7 +15,7 @@
 RING = 8
 SLOTS = 2
 CHUNKS = 3
-ORIENT = ("y", "z", "z")
+ORIENT = ("y", "z", "y")
 TILE = RING * SLOTS
 REACH = 6
 ROWS = 10
@@ -42,10 +42,9 @@
     leg_hbm,
     gain_ref,
     filt_ref,
-    start_ref,
-    width_ref,
-    order_ref,
-    order_row_ref,
+    start_hbm,
+    width_hbm,
+    order_hbm,
     ig_hbm,
     gg_ref,
     fg_ref,
@@ -60,7 +59,12 @@
     sv_slots,
     ig_slots,
     pick,
+    placed,
     out_rows,
+    start_ref,
+    width_ref,
+    order_ref,
+    order_row_ref,
     gain_mine,
     gain_got,
     gain_part,
@@ -71,7 +75,6 @@
     filt_sum,
     filt_all,
     load_sems,
-    own_sems,
     out_sems,
     p1_send,
     p1_recv,
@@ -124,12 +127,16 @@
         cp.start()
         loads[name] = cp
 
+    load("order", 8, order_hbm, order_ref)
     for c in range(CHUNKS):
         part = pl.ds(SLOTS * c, SLOTS)
         load(("og", c), 2 * c, og_hbm.at[part], og.at[part])
         load(("leg", c), 2 * c + 1, leg_hbm.at[part], leg.at[part])
     load("sp", 6, sp_hbm, sp)
     load("sv", 7, sv_hbm, sv)
+    load("row", 9, order_hbm, order_row_ref)
+    load("start", 10, start_hbm, start_ref)
+    load("width", 11, width_hbm, width_ref)
 
     barrier = pltpu.get_barrier_semaphore()
     for d in range(1, RING):
@@ -149,12 +156,12 @@
 
     degrees = sp.shape[1]
     lanes = sp.shape[2]
-    channels = gain_ref.shape[1]
+    channels = gain_ref.shape[0]
     per_channel = lanes // channels
     lat_rows = lat_count * ROWS
 
     spread = (iota((channels, lanes), 1) // per_channel == iota((channels, lanes), 0)).astype(F32)
-    lane_gain = dot(gain_ref[...], spread, precision=HIGHEST)
+    lane_gain = dot(gain_ref[...], spread, ((0,), (0,)), precision=HIGHEST)
 
     degree = iota((degrees, lanes), 0)
 
@@ -255,26 +262,27 @@
             cp.start()
         halo[c] = cps
 
+    loads["order"].wait()
+    barrier_count = 2 * (RING - 1) + 2 + lon_count - 1
     make_chunk(0)
-    pl.semaphore_wait(barrier, 2 * (RING - 1) + 2 + lon_count - 1)
+    pl.semaphore_wait(barrier, barrier_count)
     send_phase1(0)
     make_chunk(1)
     send_phase1(1)
     make_chunk(2)
-
+    send_phase1(2)
     loads["sp"].wait()
     total = jnp.zeros((degrees, lanes), F32)
     for k in range(SLOTS * CHUNKS):
         keep = degree >= order_ref[p * (SLOTS * CHUNKS) + k]
         masked = jnp.where(keep, og[k].astype(F32), 0.0)
         total = total + masked * sp[k].astype(F32)
-    groups = degrees // 64
-    packed = jnp.zeros((64, 128), F32)
-    lane_from, lane_to = iota((lanes, 128), 0), iota((lanes, 128), 1)
-    for g in range(groups):
-        fold = (lane_from // per_channel + channels * g == lane_to).astype(F32)
-        packed = packed + dot(total[64 * g : 64 * (g + 1)], fold, precision=HIGHEST)
-    gain_mine[...] = packed.reshape(RING, 8, 128)
+    terms = dot(spread, total, ((1,), (1,)), precision=HIGHEST)
+    blocks = degrees // 128
+    gain_mine[...] = jnp.zeros(gain_mine.shape, F32)
+    for h in range(channels // 8):
+        for b in range(blocks):
+            gain_mine[h * blocks + b] = terms[8 * h : 8 * h + 8, 128 * b : 128 * b + 128]
     gain1 = []
     for n, d in enumerate(FAR_FIRST):
         cp = remote(
@@ -297,7 +305,8 @@
             column = jnp.where(chunk_of == c, y_first, column)
     column = column + chunk_of * 128
     arrive = (column == iota((degrees, degrees), 1)).astype(F32)
-    order_row = jnp.broadcast_to(order_row_ref[...].astype(F32), (8, degrees))
+    loads["row"].wait()
+    order_row = jnp.broadcast_to(order_row_ref[...].reshape(1, degrees).astype(F32), (8, degrees))
     order_arrive = dot(order_row, arrive, precision=HIGHEST)[0:1]
     pick_f32 = (
         iota((degrees, degrees), 0).astype(F32) == jnp.broadcast_to(order_arrive, (degrees, degrees))
@@ -305,10 +314,6 @@
     pick[...] = pick_f32.astype(BF16)
     pick_t = pick_f32.T.astype(BF16)
 
-    turn(1)
-    send_phase2(1)
-    send_phase1(2)
-
     loads["sv"].wait()
     for j in range(0, ROWS, 2):
         pair = jnp.concatenate([sv[j], sv[j + 1]], axis=1)
@@ -317,7 +322,11 @@
         sv_slots[j + 1] = moved[:, lanes:]
 
     turn(0)
-
+    send_phase2(0)
+    turn(1)
+    send_phase2(1)
+    loads["start"].wait()
+    loads["width"].wait()
     first = p * ROWS
     e_row = iota((WINDOW, 128), 0)
     lane = iota((WINDOW, 128), 1)
@@ -331,7 +340,7 @@
     inside = (row_e >= 0) & (row_e < lat_rows) & (e_row < ROWS + 2 * REACH)
     widths = jnp.where(inside, widths, 0)
     row_pick = (iota((WINDOW, lat_rows), 1) == iota((WINDOW, lat_rows), 0) + (first - REACH)).astype(BF16)
-    taps = dot(row_pick, filt_ref[...])
+    taps = dot(row_pick, filt_ref[...], ((1,), (1,)))
     tap_count = taps.shape[1]
     tap = lane + first - starts
     band = jnp.zeros((WINDOW, 128), F32)
@@ -350,10 +359,6 @@
             (RING, WINDOW - ROWS - 2 * REACH, TILE, lanes), BF16
         )
 
-    turn(2)
-    send_phase2(2)
-    send_phase2(0)
-
     for cp in gain1:
         cp.wait_recv()
     gain_part[...] = jnp.sum(gain_got[...], axis=0)
@@ -364,23 +369,10 @@
         gain2.append(cp)
     gain_got2[y] = gain_part[...]
 
-    gram = jnp.zeros((WINDOW * TILE, ROWS * TILE), F32)
-
-    def finish_chunk(c, gram):
-        for cp in halo[c]:
-            cp.wait_recv()
-        tiles, sides = [], []
-        for t in range(RING):
-            x = window[c, t].reshape(WINDOW * TILE, lanes)
-            lo = c * 128 + t * TILE
-            ig_slots[:, lo : lo + TILE, :] = dot(band_wide, x).astype(BF16).reshape(ROWS, TILE, lanes)
-            tiles.append(x)
-            sides.append(sv_slots[:, lo : lo + TILE, :].reshape(ROWS * TILE, lanes))
-        return gram + dot(jnp.concatenate(tiles, axis=1), jnp.concatenate(sides, axis=1), ((1,), (1,)))
-
+    turn(2)
+    send_phase2(2)
+    send_halo(0)
     send_halo(1)
-    gram = finish_chunk(1, gram)
-    send_halo(0)
     for cp in gain2:
         cp.wait_recv()
     gain_mine_sum = jnp.sum(gain_got2[...], axis=0)
@@ -390,14 +382,42 @@
         cp = remote(gain_all.at[z], gain_all.at[z], g3_send.at[n], g3_recv.at[n], z_peer(d))
         cp.start()
         gain3.append(cp)
+    gram = jnp.zeros((WINDOW * TILE, ROWS * TILE), F32)
+
+    def add_gram(c, gram):
+        for cp in halo[c]:
+            cp.wait_recv()
+        tiles, sides = [], []
+        for t in range(RING):
+            lo = c * 128 + t * TILE
+            tiles.append(window[c, t].reshape(WINDOW * TILE, lanes))
+            sides.append(sv_slots[:, lo : lo + TILE, :].reshape(ROWS * TILE, lanes))
+        return gram + dot(jnp.concatenate(tiles, axis=1), jnp.concatenate(sides, axis=1), ((1,), (1,)))
+
+    def filter_rows(c):
+        for t in range(RING):
+            x = window[c, t].reshape(WINDOW * TILE, lanes)
+            lo = c * 128 + t * TILE
+            ig_slots[:, lo : lo + TILE, :] = dot(band_wide, x).astype(BF16).reshape(ROWS, TILE, lanes)
+
+    def place_rows(j, columns):
+        pair = jnp.concatenate([ig_slots[j, columns], ig_slots[j + 1, columns]], axis=1)
+        return dot(pick[:, columns], pair)
+
+    gram = add_gram(0, gram)
+    filter_rows(0)
     send_halo(2)
-    gram = finish_chunk(0, gram)
+    gram = add_gram(1, gram)
+    filter_rows(1)
+    early, late = slice(0, 256), slice(256, 384)
+    for j in range(0, ROWS, 2):
+        placed[j // 2] = place_rows(j, early)
     for cp in gain3:
         cp.wait_recv()
-    summed = gain_all[...].reshape(64, 128)
-    for g in range(groups):
-        gg_ref[64 * g : 64 * (g + 1), :] = summed[:, channels * g : channels * (g + 1)]
-    gram = finish_chunk(2, gram)
+    for h in range(channels // 8):
+        for b in range(blocks):
+            gg_ref[8 * h : 8 * h + 8, 128 * b : 128 * b + 128] = gain_all[h * blocks + b]
+    gram = add_gram(2, gram)
 
     diagonal = (iota(gram.shape, 0) & 15) == (iota(gram.shape, 1) & 15)
     gram = jnp.where(diagonal, gram, 0.0)
@@ -416,9 +436,10 @@
     for cp in filt1:
         cp.start()
 
+    filter_rows(2)
     writes = []
     for j in range(0, ROWS, 2):
-        if j == 4:
+        if j == 2:
             for cp in filt1:
                 cp.wait_recv()
             filt_sum[...] = jnp.zeros(filt_sum.shape, F32)
@@ -427,7 +448,7 @@
             filt_sum[ROWS - REACH : ROWS] += filt_got[1, 0:REACH]
             filt_all[q] = filt_sum[...]
             filt2 = []
-            for d in range(1, lon_count):
+            for d in sorted(range(1, lon_count), key=lambda d: -min(d, lon_count - d)):
                 cp = pltpu.make_async_remote_copy(
                     src_ref=filt_all.at[q],
                     dst_ref=filt_all.at[q],
@@ -438,8 +459,7 @@
                 )
                 cp.start()
                 filt2.append(cp)
-        pair = jnp.concatenate([ig_slots[j], ig_slots[j + 1]], axis=1)
-        moved = dot(pick[...], pair).astype(BF16)
+        moved = (placed[j // 2] + place_rows(j, late)).astype(BF16)
         out_rows[j] = moved[:, :lanes]
         out_rows[j + 1] = moved[:, lanes:]
         cp = pltpu.make_async_copy(
@@ -463,20 +483,19 @@
     slots, degrees, lanes = sp.shape
     rows, orders = sv.shape[0], sv.shape[1]
     lat_rows, tap_count = filt.shape
-    any_space = pl.BlockSpec(memory_space=pl.ANY)
+    hbm = pl.BlockSpec(memory_space=pltpu.HBM)
     vmem = pl.BlockSpec(memory_space=pltpu.VMEM)
-    smem = pl.BlockSpec(memory_space=pltpu.SMEM)
     dma = pltpu.SemaphoreType.DMA
     peers = RING - 1
-    return pl.pallas_call(
+    ig, gg, fg = pl.pallas_call(
         functools.partial(kernel, lon_count),
         out_shape=(
             jax.ShapeDtypeStruct(sv.shape, BF16),
-            jax.ShapeDtypeStruct(gain.shape, F32),
+            jax.ShapeDtypeStruct(gain.shape[::-1], F32),
             jax.ShapeDtypeStruct((rows, tap_count), F32),
         ),
-        in_specs=[any_space] * 4 + [vmem] * 2 + [smem] * 3 + [vmem],
-        out_specs=(any_space, vmem, vmem),
+        in_specs=[hbm] * 4 + [vmem] * 2 + [hbm] * 3,
+        out_specs=(hbm, vmem, vmem),
         scratch_shapes=[
             pltpu.VMEM(sv.shape, BF16),
             pltpu.VMEM(sp.shape, BF16),
@@ -489,7 +508,12 @@
             pltpu.VMEM((rows, orders, lanes), BF16),
             pltpu.VMEM((rows, orders, lanes), BF16),
             pltpu.VMEM((orders, orders), BF16),
+            pltpu.VMEM((rows // 2, orders, 2 * lanes), F32),
             pltpu.VMEM((rows, orders, lanes), BF16),
+            pltpu.SMEM(start.shape, I32),
+            pltpu.SMEM(width.shape, I32),
+            pltpu.SMEM(order.shape, I32),
+            pltpu.VMEM(order.shape, I32),
             pltpu.VMEM((RING, 8, 128), F32),
             pltpu.VMEM((RING, 8, 128), F32),
             pltpu.VMEM((8, 128), F32),
@@ -499,8 +523,7 @@
             pltpu.VMEM((2, WINDOW, 128), F32),
             pltpu.VMEM((16, 128), F32),
             pltpu.VMEM((lon_count, 16, 128), F32),
-            dma((8,)),
-            dma((1,)),
+            dma((12,)),
             dma((rows // 2,)),
             dma((CHUNKS, peers)),
             dma((CHUNKS, peers)),
@@ -520,10 +543,11 @@
             dma((lon_count - 1,)),
         ],
         compiler_params=pltpu.CompilerParams(
-            collective_id=0, has_side_effects=True, vmem_limit_bytes=48 * 2**20
+            collective_id=0, has_side_effects=True, vmem_limit_bytes=60 * 2**20
         ),
         name="backward",
-    )(sv, sp, og, leg, gain, filt, start, width, order, order.reshape(1, -1))
+    )(sv, sp, og, leg, gain.T, filt.T, start, width, order)
+    return ig, gg.T, fg
 
 
 def solution(mesh):

time: 95.1 us -> 85.8 us (0.902)
  local copies, waits for them, and re-layouts: 10.1 us -> 4.86 us
  Pallas kernels: 83.8 us -> 79.9 us
    pallas_call x1, Pallas kernels: 83.8 us -> 79.9 us  [per_device(): pl.pallas_call(functools.partial(kernel, lon_count), out_shape=(jax.Shape...]
    unnamed x16 -> x3, local copies, waits for them, and re-layouts: 8.69 us -> 4.86 us
where the time goes in v2:
time: 85.8 us; the launch traced here: 85.4 us
  Pallas kernels  79.9 us (93%)
  local copies, waits for them, and re-layouts  4.86 us (6%)
    pallas_call x1, Pallas kernels, per_device(): pl.pallas_call(functools.partial(kernel, lon_count), out_shape=(jax.Shape...  79.9 us
    unnamed x3, local copies, waits for them, and re-layouts  4.86 us

profile of v2, /device:TPU:1, one launch (start us, length us, event | category | flops | bytes accessed | tf_op | source)
XLA Modules:
  0.0 85.4 jit_solution(6699792493313638231)
XLA Ops:
  0.6 79.9 %backward.1 = (bf16[10,384,128]{2,1,0:T(8,128)(2,1)}, f32[16,384]{1,0:T(8,128)}, f32[10,13]{1,0:T(8,128)}) custom-call(bf16[10,384,128]{2,1,0:T(8,128)(2,1)} %sv_hbm.1, bf16[6,384,128]{2,1,0:T(8,128)(2,1)} %sp_hbm.1, bf16[6,384,128]{2,1,0:T(8,128)(2,1)} %og_hbm.1, bf16[6,384,640]{2,1,0:T(8,128)(2,1)} %leg_hbm.1, f32[16,384]{1,0:T(8,128)} %bitcast.3, ...), custom_call_target="tpu_custom_call" | custom-call | tf_op jit(solution)/shard_map/backward/pallas_call | solution.py:490
  80.6 2.2 %copy.15 = bf16[10,384,128]{2,1,0:T(8,128)(2,1)} copy(bf16[10,384,128]{2,1,0:T(8,128)(2,1)} %get-tuple-element.12) | data formatting | bytes 1966080
  82.8 1.3 %copy.16 = f32[384,16]{0,1:T(8,128)} copy(f32[384,16]{0,1:T(8,128)} %bitcast.4) | data formatting | bytes 49152
  84.1 1.3 %copy.17 = f32[10,13]{1,0:T(8,128)} copy(f32[10,13]{1,0:T(8,128)} %get-tuple-element.14) | data formatting | bytes 1040

commit v3 on v2

--- a/solution.py
+++ b/solution.py
@@ -40,7 +40,7 @@
     sp_hbm,
     og_hbm,
     leg_hbm,
-    gain_ref,
+    gain_hbm,
     filt_ref,
     start_hbm,
     width_hbm,
@@ -61,6 +61,7 @@
     pick,
     placed,
     out_rows,
+    gain_ref,
     start_ref,
     width_ref,
     order_ref,
@@ -127,16 +128,14 @@
         cp.start()
         loads[name] = cp
 
-    load("order", 8, order_hbm, order_ref)
-    for c in range(CHUNKS):
+    def load_chunk(c):
         part = pl.ds(SLOTS * c, SLOTS)
         load(("og", c), 2 * c, og_hbm.at[part], og.at[part])
         load(("leg", c), 2 * c + 1, leg_hbm.at[part], leg.at[part])
-    load("sp", 6, sp_hbm, sp)
-    load("sv", 7, sv_hbm, sv)
-    load("row", 9, order_hbm, order_row_ref)
-    load("start", 10, start_hbm, start_ref)
-    load("width", 11, width_hbm, width_ref)
+
+    load("order", 8, order_hbm, order_ref)
+    load("gain", 12, gain_hbm, gain_ref)
+    load_chunk(0)
 
     barrier = pltpu.get_barrier_semaphore()
     for d in range(1, RING):
@@ -156,11 +155,12 @@
 
     degrees = sp.shape[1]
     lanes = sp.shape[2]
-    channels = gain_ref.shape[0]
+    channels = gain_hbm.shape[0]
     per_channel = lanes // channels
     lat_rows = lat_count * ROWS
 
     spread = (iota((channels, lanes), 1) // per_channel == iota((channels, lanes), 0)).astype(F32)
+    loads["gain"].wait()
     lane_gain = dot(gain_ref[...], spread, ((0,), (0,)), precision=HIGHEST)
 
     degree = iota((degrees, lanes), 0)
@@ -179,37 +179,38 @@
 
     rows_turned = turn_rows() if "y" in ORIENT else None
 
-    def make_chunk(c):
-        loads["og", c].wait()
-        loads["leg", c].wait()
-        for s in range(SLOTS):
-            k = SLOTS * c + s
-            keep = degree >= order_ref[p * (SLOTS * CHUNKS) + k]
-            masked = jnp.where(keep, og[k].astype(F32), 0.0)
-            spec = (masked * lane_gain).astype(BF16)
-            grad = dot(leg[k], spec, ((0,), (0,))).astype(BF16)
-            if ORIENT[c] == "y":
-                grad = dot(rows_turned, grad).astype(BF16)
-            for t in range(RING):
-                sent[c, t, s] = grad[t * PLANE : (t + 1) * PLANE]
-
-    phase1 = {}
+    def make_slot(c, s):
+        k = SLOTS * c + s
+        keep = degree >= order_ref[p * (SLOTS * CHUNKS) + k]
+        masked = jnp.where(keep, og[k].astype(F32), 0.0)
+        spec = (masked * lane_gain).astype(BF16)
+        grad = dot(leg[k], spec, ((0,), (0,))).astype(BF16)
+        if ORIENT[c] == "y":
+            grad = dot(rows_turned, grad).astype(BF16)
+        for t in range(RING):
+            sent[c, t, s] = grad[t * PLANE : (t + 1) * PLANE]
+
+    phase1 = {c: [] for c in range(CHUNKS)}
     phase2 = {}
     halo = {}
 
-    def send_phase1(c):
+    def send_phase1(c, first, count):
         axis = ORIENT[c]
         me = place_of[axis]
-        cps = []
+        part = pl.ds(first, count)
         for n, d in enumerate(FAR_FIRST):
             target = lax.rem(me + d, RING)
             cp = remote(
-                sent.at[c, target], got.at[c, me], p1_send.at[c, n], p1_recv.at[c, n], peer_of[axis](d)
+                sent.at[c, target, part],
+                got.at[c, me, part],
+                p1_send.at[c, first, n],
+                p1_recv.at[c, first, n],
+                peer_of[axis](d),
             )
             cp.start()
-            cps.append(cp)
-        got[c, me] = sent[c, me]
-        phase1[c] = cps
+            phase1[c].append(cp)
+        for s in range(first, first + count):
+            got[c, me, s] = sent[c, me, s]
 
     a, b = iota((256, 256), 0), iota((256, 256), 1)
     swap = ((a & 15) * 16 + lax.shift_right_logical(a, 4) == b).astype(BF16)
@@ -240,37 +241,55 @@
         phase2[c] = cps
 
     def send_halo(c):
-        for cp in phase2[c]:
-            cp.wait_recv()
-        cps = [
-            remote(
-                window.at[c, :, pl.ds(ROWS, REACH)],
-                window.at[c, :, pl.ds(0, REACH)],
-                halo_send.at[c, 0],
-                halo_recv.at[c, 0],
-                up,
-            ),
-            remote(
-                window.at[c, :, pl.ds(REACH, REACH)],
-                window.at[c, :, pl.ds(REACH + ROWS, REACH)],
-                halo_send.at[c, 1],
-                halo_recv.at[c, 1],
-                down,
-            ),
-        ]
-        for cp in cps:
-            cp.start()
+        me = place_of[other[ORIENT[c]]]
+        cps = []
+        for n in range(RING):
+            tile = me
+            if n:
+                phase2[c][n - 1].wait_recv()
+                tile = lax.rem(me + RING - FAR_FIRST[n - 1], RING)
+            cps += [
+                remote(
+                    window.at[c, tile, pl.ds(ROWS, REACH)],
+                    window.at[c, tile, pl.ds(0, REACH)],
+                    halo_send.at[c, 0, n],
+                    halo_recv.at[c, 0, n],
+                    up,
+                ),
+                remote(
+                    window.at[c, tile, pl.ds(REACH, REACH)],
+                    window.at[c, tile, pl.ds(REACH + ROWS, REACH)],
+                    halo_send.at[c, 1, n],
+                    halo_recv.at[c, 1, n],
+                    down,
+                ),
+            ]
+            for cp in cps[-2:]:
+                cp.start()
         halo[c] = cps
 
     loads["order"].wait()
-    barrier_count = 2 * (RING - 1) + 2 + lon_count - 1
-    make_chunk(0)
-    pl.semaphore_wait(barrier, barrier_count)
-    send_phase1(0)
-    make_chunk(1)
-    send_phase1(1)
-    make_chunk(2)
-    send_phase1(2)
+    loads["og", 0].wait()
+    loads["leg", 0].wait()
+    for c in range(1, CHUNKS):
+        load_chunk(c)
+    load("sp", 6, sp_hbm, sp)
+    load("sv", 7, sv_hbm, sv)
+    load("row", 9, order_hbm, order_row_ref)
+    load("start", 10, start_hbm, start_ref)
+    load("width", 11, width_hbm, width_ref)
+    make_slot(0, 0)
+    pl.semaphore_wait(barrier, 2 * (RING - 1) + 2 + lon_count - 1)
+    send_phase1(0, 0, 1)
+    make_slot(0, 1)
+    send_phase1(0, 1, 1)
+    for c in range(1, CHUNKS):
+        loads["og", c].wait()
+        loads["leg", c].wait()
+        for s in range(SLOTS):
+            make_slot(c, s)
+        send_phase1(c, 0, SLOTS)
+
     loads["sp"].wait()
     total = jnp.zeros((degrees, lanes), F32)
     for k in range(SLOTS * CHUNKS):
@@ -446,7 +465,7 @@
             filt_sum[0:ROWS] = filt_mine[REACH : REACH + ROWS]
             filt_sum[0:REACH] += filt_got[0, REACH + ROWS : ROWS + 2 * REACH]
             filt_sum[ROWS - REACH : ROWS] += filt_got[1, 0:REACH]
-            filt_all[q] = filt_sum[...]
+            filt_all[q] = filt_sum[0:8] + pltpu.roll(filt_sum[8:16], 64, 1)
             filt2 = []
             for d in sorted(range(1, lon_count), key=lambda d: -min(d, lon_count - d)):
                 cp = pltpu.make_async_remote_copy(
@@ -470,7 +489,9 @@
 
     for cp in filt2:
         cp.wait_recv()
-    fg_ref[...] = jnp.sum(filt_all[...], axis=0)[:ROWS, :tap_count]
+    filt_total = jnp.sum(filt_all[...], axis=0)
+    fg_ref[0:8] = filt_total[:, :tap_count]
+    fg_ref[8:ROWS] = filt_total[: ROWS - 8, 64 : 64 + tap_count]
     for cps in [*phase1.values(), *phase2.values(), *halo.values(), gain1, gain2, gain3, filt1, filt2]:
         for cp in cps:
             cp.wait_send()
@@ -494,7 +515,7 @@
             jax.ShapeDtypeStruct(gain.shape[::-1], F32),
             jax.ShapeDtypeStruct((rows, tap_count), F32),
         ),
-        in_specs=[hbm] * 4 + [vmem] * 2 + [hbm] * 3,
+        in_specs=[hbm] * 5 + [vmem] + [hbm] * 3,
         out_specs=(hbm, vmem, vmem),
         scratch_shapes=[
             pltpu.VMEM(sv.shape, BF16),
@@ -510,6 +531,7 @@
             pltpu.VMEM((orders, orders), BF16),
             pltpu.VMEM((rows // 2, orders, 2 * lanes), F32),
             pltpu.VMEM((rows, orders, lanes), BF16),
+            pltpu.VMEM(gain.shape[::-1], F32),
             pltpu.SMEM(start.shape, I32),
             pltpu.SMEM(width.shape, I32),
             pltpu.SMEM(order.shape, I32),
@@ -522,15 +544,15 @@
             pltpu.VMEM((WINDOW, 128), F32),
             pltpu.VMEM((2, WINDOW, 128), F32),
             pltpu.VMEM((16, 128), F32),
-            pltpu.VMEM((lon_count, 16, 128), F32),
-            dma((12,)),
+            pltpu.VMEM((lon_count, 8, 128), F32),
+            dma((13,)),
             dma((rows // 2,)),
+            dma((CHUNKS, SLOTS, peers)),
+            dma((CHUNKS, SLOTS, peers)),
             dma((CHUNKS, peers)),
             dma((CHUNKS, peers)),
-            dma((CHUNKS, peers)),
-            dma((CHUNKS, peers)),
-            dma((CHUNKS, 2)),
-            dma((CHUNKS, 2)),
+            dma((CHUNKS, 2, RING)),
+            dma((CHUNKS, 2, RING)),
             dma((peers,)),
             dma((peers,)),
             dma((peers,)),

time: 85.8 us -> 85.1 us (level)
  no operation moved by 1% of the time
where the time goes in v3:
time: 85.1 us; the launch traced here: 84.8 us
  Pallas kernels  79.3 us (93%)
  local copies, waits for them, and re-layouts  4.86 us (6%)
    pallas_call x1, Pallas kernels, per_device(): pl.pallas_call(functools.partial(kernel, lon_count), out_shape=(jax.Shape...  79.3 us
    unnamed x3, local copies, waits for them, and re-layouts  4.86 us

profile of v3, /device:TPU:1, one launch (start us, length us, event | category | flops | bytes accessed | tf_op | source)
XLA Modules:
  0.0 84.8 jit_solution(1417436898644562159)
XLA Ops:
  0.6 79.3 %backward.1 = (bf16[10,384,128]{2,1,0:T(8,128)(2,1)}, f32[16,384]{1,0:T(8,128)}, f32[10,13]{1,0:T(8,128)}) custom-call(bf16[10,384,128]{2,1,0:T(8,128)(2,1)} %sv_hbm.1, bf16[6,384,128]{2,1,0:T(8,128)(2,1)} %sp_hbm.1, bf16[6,384,128]{2,1,0:T(8,128)(2,1)} %og_hbm.1, bf16[6,384,640]{2,1,0:T(8,128)(2,1)} %leg_hbm.1, f32[16,384]{1,0:T(8,128)} %bitcast.3, ...), custom_call_target="tpu_custom_call" | custom-call | tf_op jit(solution)/shard_map/backward/pallas_call | solution.py:511
  79.9 2.2 %copy.15 = bf16[10,384,128]{2,1,0:T(8,128)(2,1)} copy(bf16[10,384,128]{2,1,0:T(8,128)(2,1)} %get-tuple-element.12) | data formatting | bytes 1966080
  82.1 1.3 %copy.16 = f32[384,16]{0,1:T(8,128)} copy(f32[384,16]{0,1:T(8,128)} %bitcast.4) | data formatting | bytes 49152
  83.5 1.3 %copy.17 = f32[10,13]{1,0:T(8,128)} copy(f32[10,13]{1,0:T(8,128)} %get-tuple-element.14) | data formatting | bytes 1040
